TPU v7x, 32 devices: a whole 2x2x4 slice. The times are simulated.
32 devices in a mesh: pb: 8 (over y, x, core), row: 4 (over z).
Axes of the slice: x: 2, y: 2, z: 4, core: 2. Of those that a mesh axis runs over, the one named last changes fastest.
Arguments:
- query_emb: bfloat16 [16384, 512], P(('pb', 'row')), may hold values from -4 to 4
- query_scales: float32 [16384, 4], P(('pb', 'row')), may hold values from 0.25 to 4
- sharpness: float32 [16384], P(('pb', 'row')), may hold values from 4 to 400
- ref_emb: bfloat16 [32768, 512], P(('pb', 'row')), may hold values from -4 to 4
- ref_scales: float32 [32768, 4], P(('pb', 'row')), may hold values from 0.25 to 4
- properties: bfloat16 [32768, 128], P(('pb', 'row')), may hold values from -4 to 4
- band_mask: int32 [64, 128], P(('pb', 'row')), may hold values from 0 to 1, as said below
- ref_skew: int32 [8], replicated, may hold values from 0 to 3, as said below
Outputs:
- transferred: float32 [16384, 128], P(('pb', 'row'))
Inputs may be any that keep to these rules, and one draw needn't show every extreme that they name: `band_mask`: for k = p * 4 + r, every tile of query rows of block k has a 1 against some tile of reference block p * 4 + ((r - ref_skew[p]) mod 4). `ref_skew`: every value from 0 to 3 occurs.
All inputs are finite; a program needn't handle non-finite values.
Results may differ from a plain program's by a relative error of at most 0.007.
Values may be sent and summed in bfloat16 or wider, within the bound.
A program may use at most 64 MiB of HBM per device.

v0:
```python
import jax
import jax.numpy as jnp
from jax import lax
from jax.sharding import PartitionSpec as P

STEPS = 4
SKEW_BITS = 4


EPSILON = 1e-06
FLOOR = -1e30


def shifted(value, axis, steps):
    count = lax.axis_size(axis)
    pairs = [(source, (source + steps) % count) for source in range(count)]
    return lax.ppermute(value, axis, pairs)


def dequantize(values, scales):
    row_count, column_count = values.shape
    groups = scales.shape[1]
    widened = (
        values.astype(jnp.float32).reshape(row_count, groups, column_count // groups)
        * scales[:, :, None]
    )
    return widened.reshape(row_count, column_count).astype(jnp.bfloat16)


def squares(matrix):
    return jnp.sum(jnp.square(matrix.astype(jnp.float32)), axis=1)


def visit(carried, queries, query_sq, sharpen, references, props, counted_tiles, tile_rows):
    run_max, run_sum, weighted = carried
    reference_sq = squares(references)
    products = lax.dot_general(
        queries, references, (((1,), (1,)), ((), ())), preferred_element_type=jnp.float32
    )
    scores = (
        sharpen[:, None]
        * products
        / (query_sq[:, None] + reference_sq[None, :] - products + EPSILON)
    )
    query_tiles, ref_tiles = counted_tiles.shape
    counted = jnp.broadcast_to(
        counted_tiles[:, None, :, None], (query_tiles, tile_rows, ref_tiles, tile_rows)
    )
    counted = counted.reshape(query_tiles * tile_rows, ref_tiles * tile_rows)
    new_max = jnp.maximum(run_max, jnp.max(jnp.where(counted, scores, FLOOR), axis=1))
    rescale = jnp.exp(run_max - new_max)
    weights = jnp.where(counted, jnp.exp(scores - new_max[:, None]), 0.0)
    run_sum = rescale * run_sum + jnp.sum(weights, axis=1)
    weighted = rescale[:, None] * weighted + jnp.dot(
        weights.astype(jnp.bfloat16), props, preferred_element_type=jnp.float32
    )
    return (new_max, run_sum, weighted)


def local(query_emb, query_scales, sharpness, ref_emb, ref_scales, properties, band_mask, ref_skew):
    pb_count = lax.axis_size("pb")
    row_count = lax.axis_size("row")
    pb_place = lax.axis_index("pb")
    row_place = lax.axis_index("row")
    query_total = query_emb.shape[0]
    tile_rows = query_total // band_mask.shape[0]
    ref_tiles = ref_emb.shape[0] // tile_rows
    queries = dequantize(query_emb, query_scales)
    query_sq = squares(queries)
    reference_block = (dequantize(ref_emb, ref_scales), properties)
    offset = ref_skew[pb_place]
    for binary_place in range(SKEW_BITS):
        incoming = shifted((reference_block[0], reference_block[1]), "row", 1 << binary_place)
        chosen = offset // (1 << binary_place) % 2 == 1
        reference_block = (
            jnp.where(chosen, incoming[0], reference_block[0]),
            jnp.where(chosen, incoming[1], reference_block[1]),
        )
    tile_lists = []
    for turn_index in range(STEPS):
        pb_group = (pb_place + turn_index) % pb_count
        row_slot = (row_place - ref_skew[pb_group] - turn_index) % row_count
        visited = pb_group * row_count + row_slot
        tile_lists.append(lax.dynamic_slice_in_dim(band_mask, visited * ref_tiles, ref_tiles, 1))
    flagged = jnp.stack(tile_lists).astype(jnp.float32)
    carried = (
        jnp.full((query_total,), FLOOR, jnp.float32),
        jnp.zeros((query_total,), jnp.float32),
        jnp.zeros((query_total, properties.shape[1]), jnp.float32),
    )
    moving = queries
    extras = (query_sq, sharpness, flagged) + carried
    for turn_index in range(STEPS):
        carried = visit(
            extras[3:],
            moving,
            extras[0],
            extras[1],
            reference_block[0],
            reference_block[1],
            extras[2][turn_index] > 0.5,
            tile_rows,
        )
        extras = extras[:3] + carried
        if turn_index + 1 < STEPS:
            moving = shifted(moving, "pb", 1)
            extras = shifted(extras, "pb", 1)
            reference_block = shifted((reference_block[0], reference_block[1]), "row", 1)
    finished = extras[5] / extras[4][:, None]
    return shifted(finished, "pb", 1 - STEPS)


def solution(mesh):
    placed = (
        P(("pb", "row"), None),
        P(("pb", "row"), None),
        P(("pb", "row")),
        P(("pb", "row"), None),
        P(("pb", "row"), None),
        P(("pb", "row"), None),
        P(("pb", "row"), None),
        P(),
    )
    return jax.shard_map(
        local, mesh=mesh, in_specs=placed, out_specs=P(("pb", "row"), None), check_vma=False
    )
```

profile of v0, /device:TPU:0, one launch (start us, length us, event | category | flops | bytes accessed | tf_op | source)
XLA Modules:
  0.0 216.2 jit_solution(2149991299438034665)
XLA Ops:
  0.0 1.0 copy.10
  1.0 1.2 mul.133
  2.3 0.4 fusion
  2.7 3.1 %collective-permute-start = (bf16[1024,512]{1,0:T(8,128)(2,1)S(1)}, bf16[1024,512]{1,0:T(8,128)(2,1)S(1)}, u32[]{:S(2)}, u32[]{:S(2)}) collective-permute-start(bf16[1024,512]{1,0:T(8,128)(2,1)S(1)} %fusion), channel_id=1, source_target_pairs={{0,1},{1,2},{2,3},{3,0},{4,5},{5,6},{6,7},{7,4},{8,9},{9,10},{10,1... | collective-permute-start | bytes 3145736 | tf_op jit(solution)/shard_map/ppermute | solution.py:17
  5.8 0.7 fusion.32
  8.4 22.6 %collective-permute-done = bf16[1024,512]{1,0:T(8,128)(2,1)S(1)} collective-permute-done((bf16[1024,512]{1,0:T(8,128)(2,1)S(1)}, bf16[1024,512]{1,0:T(8,128)(2,1)S(1)}, u32[]{:S(2)}, u32[]{:S(2)}) %collective-permute-start) | collective-permute-done | bytes 1048608 | tf_op jit(solution)/shard_map/ppermute | solution.py:17
  31.1 0.8 collective-permute-start.1
  31.9 1.6 collective-permute-start.22
  36.9 46.5 %collective-permute-done.1 = bf16[1024,512]{1,0:T(8,128)(2,1)S(1)} collective-permute-done((bf16[1024,512]{1,0:T(8,128)(2,1)S(1)}, bf16[1024,512]{1,0:T(8,128)(2,1)S(1)}, u32[]{:S(2)}, u32[]{:S(2)}) %collective-permute-start.1) | collective-permute-done | bytes 1048608 | tf_op jit(solution)/shard_map/ppermute | solution.py:17
  83.9 1.3 collective-permute-start.23
  85.1 0.6 mul.130
  85.7 2.0 multiply_reduce_fusion.4
  87.7 1.3 collective-permute-start.7
  89.3 0.3 broadcast_in_dim.25
  90.0 8.2 %collective-permute-done.23 = bf16[1024,128]{1,0:T(8,128)(2,1)S(1)} collective-permute-done((bf16[1024,128]{1,0:T(8,128)(2,1)S(1)}, bf16[1024,128]{1,0:T(8,128)(2,1)S(1)}, u32[]{:S(2)}, u32[]{:S(2)}) %collective-permute-start.23) | collective-permute-done | bytes 262176 | tf_op jit(solution)/shard_map/ppermute | solution.py:17
  98.5 0.3 broadcast_in_dim.28
  99.3 3.8 %collective-permute-done.11 = f32[4,2,4]{2,1,0:T(2,128)S(1)} collective-permute-done((f32[4,2,4]{2,1,0:T(2,128)S(1)}, f32[4,2,4]{2,1,0:T(2,128)S(1)}, u32[]{:S(2)}, u32[]{:S(2)}) %collective-permute-start.11) | collective-permute-done | bytes 160 | tf_op jit(solution)/shard_map/ppermute | solution.py:17
  103.1 0.3 broadcast_in_dim.29
  103.7 3.3 %collective-permute-done.17 = f32[4,2,4]{2,1,0:T(2,128)S(1)} collective-permute-done((f32[4,2,4]{2,1,0:T(2,128)S(1)}, f32[4,2,4]{2,1,0:T(2,128)S(1)}, u32[]{:S(2)}, u32[]{:S(2)}) %collective-permute-start.17) | collective-permute-done | bytes 160 | tf_op jit(solution)/shard_map/ppermute | solution.py:17
  107.0 0.3 broadcast_in_dim.30
  107.8 0.4 multiply_reduce_fusion.3
  108.4 2.2 %select_reduce_fusion.3 = (f32[512]{0:T(512)S(1)}, f32[512,1024]{1,0:T(8,128)S(1)}) fusion(pred[512,1024]{1,0:T(8,128)(4,1)S(1)} %bitcast.67, f32[1024]{0:T(1024)S(1)} %get-tuple-element.19, f32[512]{0:T(512)S(1)} %get-tuple-element.21, f32[512]{0:T(512)S(1)} %copy-done.5, bf16[512,512]{1,0:T(8,128)(2,1)} %get-tuple-element.22, ...), kind=kOutput, calls=%fused_computation.15 | convolution fusion | flops 540540416 | bytes 4204544 | tf_op jit(solution)/shard_map/dot_general | solution.py:37
  110.6 0.7 fusion.1
  111.3 0.6 convolution_add_fusion.2
  111.9 28.2 %collective-permute-done.8 = bf16[1024,512]{1,0:T(8,128)(2,1)S(1)} collective-permute-done((bf16[1024,512]{1,0:T(8,128)(2,1)S(1)}, bf16[1024,512]{1,0:T(8,128)(2,1)S(1)}, u32[]{:S(2)}, u32[]{:S(2)}) %collective-permute-start.8) | collective-permute-done | bytes 1048608 | tf_op jit(solution)/shard_map/ppermute | solution.py:17
  140.4 2.5 %collective-permute-start.32 = (f32[512]{0:T(512)S(1)}, f32[512]{0:T(512)S(1)}, u32[]{:S(2)}, u32[]{:S(2)}) collective-permute-start(f32[512]{0:T(512)S(1)} %get-tuple-element.23), channel_id=1, source_target_pairs={{0,4},{4,8},{8,12},{12,16},{16,20},{20,24},{24,28},{28,0},{1,5},{5... | collective-permute-start | bytes 6152 | tf_op jit(solution)/shard_map/ppermute | solution.py:17
  142.9 2.2 %select_reduce_fusion.2 = (f32[512]{0:T(512)S(1)}, f32[512,1024]{1,0:T(8,128)S(1)}) fusion(pred[512,1024]{1,0:T(8,128)(4,1)S(1)} %bitcast.64, f32[1024]{0:T(1024)S(1)} %multiply_reduce_fusion.2, f32[512]{0:T(512)S(1)} %collective-permute-done.9, f32[512]{0:T(512)S(1)} %collective-permute-done.6, bf16[512,512]{1,0:T(8,128)(2,1)} %collective-permute-done.7, ...), kind=kOutput, calls=%fused_computation.12 | convolution fusion | flops 540540416 | bytes 4204544 | tf_op jit(solution)/shard_map/dot_general | solution.py:37
  145.3 0.6 fusion.3
  145.9 0.8 collective-permute-start.13
  146.9 2.2 %collective-permute-start.21 = (f32[512]{0:T(512)S(1)}, f32[512]{0:T(512)S(1)}, u32[]{:S(2)}, u32[]{:S(2)}) collective-permute-start(f32[512]{0:T(512)S(1)} %collective-permute-done.15), channel_id=1, source_target_pairs={{0,4},{4,8},{8,12},{12,16},{16,20},{20,24},{24,28},{28,0},{1,5},{5... | collective-permute-start | bytes 6152 | tf_op jit(solution)/shard_map/ppermute | solution.py:17
  149.1 2.8 %collective-permute-done.26 = f32[512,128]{1,0:T(8,128)S(1)} collective-permute-done((f32[512,128]{1,0:T(8,128)S(1)}, f32[512,128]{1,0:T(8,128)S(1)}, u32[]{:S(2)}, u32[]{:S(2)}) %collective-permute-start.26) | collective-permute-done | bytes 262176 | tf_op jit(solution)/shard_map/ppermute | solution.py:17
  151.9 0.6 multiply_add_fusion
  152.5 18.2 %collective-permute-done.14 = bf16[1024,512]{1,0:T(8,128)(2,1)S(1)} collective-permute-done((bf16[1024,512]{1,0:T(8,128)(2,1)S(1)}, bf16[1024,512]{1,0:T(8,128)(2,1)S(1)}, u32[]{:S(2)}, u32[]{:S(2)}) %collective-permute-start.14) | collective-permute-done | bytes 1048608 | tf_op jit(solution)/shard_map/ppermute | solution.py:17
  171.0 0.9 collective-permute-start.33
  171.9 1.2 select_reduce_fusion.1
  173.1 1.6 collective-permute-done.10
  174.6 0.6 fusion.5
  175.3 0.9 collective-permute-start.19
  176.3 5.0 %collective-permute-done.28 = f32[512,128]{1,0:T(8,128)S(1)} collective-permute-done((f32[512,128]{1,0:T(8,128)S(1)}, f32[512,128]{1,0:T(8,128)S(1)}, u32[]{:S(2)}, u32[]{:S(2)}) %collective-permute-start.28) | collective-permute-done | bytes 262176 | tf_op jit(solution)/shard_map/ppermute | solution.py:17
  181.3 0.6 convolution_add_fusion.1
  181.9 17.8 %collective-permute-done.20 = bf16[1024,512]{1,0:T(8,128)(2,1)S(1)} collective-permute-done((bf16[1024,512]{1,0:T(8,128)(2,1)S(1)}, bf16[1024,512]{1,0:T(8,128)(2,1)S(1)}, u32[]{:S(2)}, u32[]{:S(2)}) %collective-permute-start.20) | collective-permute-done | bytes 1048608 | tf_op jit(solution)/shard_map/ppermute | solution.py:17
  200.0 2.3 %collective-permute-start.34 = (f32[512]{0:T(512)S(1)}, f32[512]{0:T(512)S(1)}, u32[]{:S(2)}, u32[]{:S(2)}) collective-permute-start(f32[512]{0:T(512)S(1)} %get-tuple-element.7), channel_id=1, source_target_pairs={{0,4},{4,8},{8,12},{12,16},{16,20},{20,24},{24,28},{28,0},{1,5},{5... | collective-permute-start | bytes 6152 | tf_op jit(solution)/shard_map/ppermute | solution.py:17
  202.4 1.2 select_reduce_fusion
  203.6 0.6 fusion.7
  204.4 4.6 %collective-permute-done.30 = f32[512,128]{1,0:T(8,128)S(1)} collective-permute-done((f32[512,128]{1,0:T(8,128)S(1)}, f32[512,128]{1,0:T(8,128)S(1)}, u32[]{:S(2)}, u32[]{:S(2)}) %collective-permute-start.30) | collective-permute-done | bytes 262176 | tf_op jit(solution)/shard_map/ppermute | solution.py:17
  209.0 0.6 fusion.9
  209.7 5.8 %collective-permute-done.35 = f32[512,128]{1,0:T(8,128)S(1)} collective-permute-done((f32[512,128]{1,0:T(8,128)S(1)}, f32[512,128]{1,0:T(8,128)S(1)}, u32[]{:S(2)}, u32[]{:S(2)}) %collective-permute-start.35) | collective-permute-done | bytes 262176 | tf_op jit(solution)/shard_map/ppermute | solution.py:17
  215.5 0.7 copy.21
  (89 shorter events, 4.4 us)
Async XLA Ops:
  0.0 2.3 %copy-start = (bf16[1024,512]{1,0:T(8,128)(2,1)S(1)}, bf16[1024,512]{1,0:T(8,128)(2,1)}, u32[]{:S(2)}) copy-start(bf16[1024,512]{1,0:T(8,128)(2,1)} %param.11) | copy-start | bytes 3145732
  2.3 3.5 %copy-start.3 = (s32[8]{0:T(128)S(1)}, s32[8]{0:T(128)}, u32[]{:S(2)}) copy-start(s32[8]{0:T(128)} %param.15) | copy-start | bytes 100
  2.7 29.2 %copy-start.1 = (bf16[1024,128]{1,0:T(8,128)(2,1)S(1)}, bf16[1024,128]{1,0:T(8,128)(2,1)}, u32[]{:S(2)}) copy-start(bf16[1024,128]{1,0:T(8,128)(2,1)} %param.13) | copy-start | bytes 786436
  2.7 34.1 %copy-start.2 = (s32[2,128]{1,0:T(2,128)S(1)}, s32[2,128]{1,0:T(2,128)}, u32[]{:S(2)}) copy-start(s32[2,128]{1,0:T(2,128)} %param.14) | copy-start | bytes 3076
  2.7 28.3 %collective-permute-start = (bf16[1024,512]{1,0:T(8,128)(2,1)S(1)}, bf16[1024,512]{1,0:T(8,128)(2,1)S(1)}, u32[]{:S(2)}, u32[]{:S(2)}) collective-permute-start(bf16[1024,512]{1,0:T(8,128)(2,1)S(1)} %fusion), channel_id=1, source_target_pairs={{0,1},{1,2},{2,3},{3,0},{4,5},{5,6},{6,7},{7,4},{8,9},{9,10},{10,1... | collective-permute-start | bytes 3145736 | tf_op jit(solution)/shard_map/ppermute | solution.py:17
  31.1 52.5 %copy-start.4 = (f32[512,4]{0,1:T(4,128)S(1)}, f32[512,4]{0,1:T(4,128)}, u32[]{:S(2)}) copy-start(f32[512,4]{0,1:T(4,128)} %param.9) | copy-start | bytes 24580
  31.1 52.2 %collective-permute-start.1 = (bf16[1024,512]{1,0:T(8,128)(2,1)S(1)}, bf16[1024,512]{1,0:T(8,128)(2,1)S(1)}, u32[]{:S(2)}, u32[]{:S(2)}) collective-permute-start(bf16[1024,512]{1,0:T(8,128)(2,1)S(1)} %broadcast_select_fusion), channel_id=1, source_target_pairs={{0,2},{1,3},{2,0},{3,1},{4,6},{5,7},{6,4},{7,5},{8,10},{9,11},{10,... | collective-permute-start | bytes 3145736 | tf_op jit(solution)/shard_map/ppermute | solution.py:17
  31.9 51.9 %collective-permute-start.22 = (bf16[1024,128]{1,0:T(8,128)(2,1)S(1)}, bf16[1024,128]{1,0:T(8,128)(2,1)}, u32[]{:S(2)}, u32[]{:S(2)}) collective-permute-start(bf16[1024,128]{1,0:T(8,128)(2,1)S(1)} %copy-done.1), channel_id=1, source_target_pairs={{0,1},{1,2},{2,3},{3,0},{4,5},{5,6},{6,7},{7,4},{8,9},{9,10},{10,1... | collective-permute-start | bytes 786440 | tf_op jit(solution)/shard_map/ppermute | solution.py:17
  83.5 14.7 %collective-permute-start.2 = (bf16[1024,512]{1,0:T(8,128)(2,1)S(1)}, bf16[1024,512]{1,0:T(8,128)(2,1)S(1)}, u32[]{:S(2)}, u32[]{:S(2)}) collective-permute-start(bf16[1024,512]{1,0:T(8,128)(2,1)S(1)} %broadcast_select_fusion.1), channel_id=1, source_target_pairs={{0,0},{1,1},{2,2},{3,3},{4,4},{5,5},{6,6},{7,7},{8,8},{9,9},{10,10... | collective-permute-start | bytes 3145736 | tf_op jit(solution)/shard_map/ppermute | solution.py:17
  83.6 14.9 %collective-permute-start.5 = (f32[4,2,4]{2,1,0:T(2,128)S(1)}, f32[4,2,4]{2,1,0:T(2,128)S(1)}, u32[]{:S(2)}, u32[]{:S(2)}) collective-permute-start(f32[4,2,4]{2,1,0:T(2,128)S(1)} %add_convert_fusion), channel_id=1, source_target_pairs={{0,4},{4,8},{8,12},{12,16},{16,20},{20,24},{24,28},{28,0},{1,5},{5... | collective-permute-start | bytes 392 | tf_op jit(solution)/shard_map/ppermute | solution.py:17
  83.9 14.3 %collective-permute-start.23 = (bf16[1024,128]{1,0:T(8,128)(2,1)S(1)}, bf16[1024,128]{1,0:T(8,128)(2,1)S(1)}, u32[]{:S(2)}, u32[]{:S(2)}) collective-permute-start(bf16[1024,128]{1,0:T(8,128)(2,1)S(1)} %broadcast_select_fusion.4), channel_id=1, source_target_pairs={{0,2},{1,3},{2,0},{3,1},{4,6},{5,7},{6,4},{7,5},{8,10},{9,11},{10,... | collective-permute-start | bytes 786440 | tf_op jit(solution)/shard_map/ppermute | solution.py:17
  87.7 55.2 %collective-permute-start.7 = (bf16[512,512]{1,0:T(8,128)(2,1)}, bf16[512,512]{1,0:T(8,128)(2,1)}, u32[]{:S(2)}, u32[]{:S(2)}) collective-permute-start(bf16[512,512]{1,0:T(8,128)(2,1)} %get-tuple-element.22), channel_id=1, source_target_pairs={{0,4},{4,8},{8,12},{12,16},{16,20},{20,24},{24,28},{28,0},{1,5},{5... | collective-permute-start | bytes 1572872 | tf_op jit(solution)/shard_map/ppermute | solution.py:17
  89.0 18.6 %collective-permute-start.9 = (f32[512]{0:T(512)S(1)}, f32[512]{0:T(512)S(1)}, u32[]{:S(2)}, u32[]{:S(2)}) collective-permute-start(f32[512]{0:T(512)S(1)} %get-tuple-element.21), channel_id=1, source_target_pairs={{0,4},{4,8},{8,12},{12,16},{16,20},{20,24},{24,28},{28,0},{1,5},{5... | collective-permute-start | bytes 6152 | tf_op jit(solution)/shard_map/ppermute | solution.py:17
  98.2 1.1 collective-permute-start.24
  98.3 8.7 %copy-start.5 = (f32[512]{0:T(512)S(1)}, f32[512]{0:T(512)}, u32[]{:S(2)}) copy-start(f32[512]{0:T(512)} %param.10) | copy-start | bytes 6148
  98.3 9.5 %collective-permute-start.3 = (bf16[1024,512]{1,0:T(8,128)(2,1)S(1)}, bf16[1024,512]{1,0:T(8,128)(2,1)S(1)}, u32[]{:S(2)}, u32[]{:S(2)}) collective-permute-start(bf16[1024,512]{1,0:T(8,128)(2,1)S(1)} %broadcast_select_fusion.2), channel_id=1, source_target_pairs={{0,0},{1,1},{2,2},{3,3},{4,4},{5,5},{6,6},{7,7},{8,8},{9,9},{10,10... | collective-permute-start | bytes 3145736 | tf_op jit(solution)/shard_map/ppermute | solution.py:17
  99.1 4.0 %collective-permute-start.11 = (f32[4,2,4]{2,1,0:T(2,128)S(1)}, f32[4,2,4]{2,1,0:T(2,128)S(1)}, u32[]{:S(2)}, u32[]{:S(2)}) collective-permute-start(f32[4,2,4]{2,1,0:T(2,128)S(1)} %collective-permute-done.5), channel_id=1, source_target_pairs={{0,4},{4,8},{8,12},{12,16},{16,20},{20,24},{24,28},{28,0},{1,5},{5... | collective-permute-start | bytes 392 | tf_op jit(solution)/shard_map/ppermute | solution.py:17
  99.3 8.4 %collective-permute-start.25 = (bf16[1024,128]{1,0:T(8,128)(2,1)S(1)}, bf16[1024,128]{1,0:T(8,128)(2,1)S(1)}, u32[]{:S(2)}, u32[]{:S(2)}) collective-permute-start(bf16[1024,128]{1,0:T(8,128)(2,1)S(1)} %broadcast_select_fusion.6), channel_id=1, source_target_pairs={{0,0},{1,1},{2,2},{3,3},{4,4},{5,5},{6,6},{7,7},{8,8},{9,9},{10,10... | collective-permute-start | bytes 786440 | tf_op jit(solution)/shard_map/ppermute | solution.py:17
  103.1 3.9 %collective-permute-start.17 = (f32[4,2,4]{2,1,0:T(2,128)S(1)}, f32[4,2,4]{2,1,0:T(2,128)S(1)}, u32[]{:S(2)}, u32[]{:S(2)}) collective-permute-start(f32[4,2,4]{2,1,0:T(2,128)S(1)} %collective-permute-done.11), channel_id=1, source_target_pairs={{0,4},{4,8},{8,12},{12,16},{16,20},{20,24},{24,28},{28,0},{1,5},{5... | collective-permute-start | bytes 392 | tf_op jit(solution)/shard_map/ppermute | solution.py:17
  107.0 33.4 %collective-permute-start.6 = (f32[512]{0:T(512)S(1)}, f32[512]{0:T(512)S(1)}, u32[]{:S(2)}, u32[]{:S(2)}) collective-permute-start(f32[512]{0:T(512)S(1)} %copy-done.5), channel_id=1, source_target_pairs={{0,4},{4,8},{8,12},{12,16},{16,20},{20,24},{24,28},{28,0},{1,5},{5... | collective-permute-start | bytes 6152 | tf_op jit(solution)/shard_map/ppermute | solution.py:17
  107.6 39.1 %collective-permute-start.15 = (f32[512]{0:T(512)S(1)}, f32[512]{0:T(512)S(1)}, u32[]{:S(2)}, u32[]{:S(2)}) collective-permute-start(f32[512]{0:T(512)S(1)} %collective-permute-done.9), channel_id=1, source_target_pairs={{0,4},{4,8},{8,12},{12,16},{16,20},{20,24},{24,28},{28,0},{1,5},{5... | collective-permute-start | bytes 6152 | tf_op jit(solution)/shard_map/ppermute | solution.py:17
  107.7 39.1 %collective-permute-start.27 = (bf16[1024,128]{1,0:T(8,128)(2,1)S(1)}, bf16[1024,128]{1,0:T(8,128)(2,1)S(1)}, u32[]{:S(2)}, u32[]{:S(2)}) collective-permute-start(bf16[1024,128]{1,0:T(8,128)(2,1)S(1)} %broadcast_select_fusion.7), channel_id=1, source_target_pairs={{0,1},{1,2},{2,3},{3,0},{4,5},{5,6},{6,7},{7,4},{8,9},{9,10},{10,1... | collective-permute-start | bytes 786440 | tf_op jit(solution)/shard_map/ppermute | solution.py:17
  108.3 31.8 %collective-permute-start.8 = (bf16[1024,512]{1,0:T(8,128)(2,1)S(1)}, bf16[1024,512]{1,0:T(8,128)(2,1)S(1)}, u32[]{:S(2)}, u32[]{:S(2)}) collective-permute-start(bf16[1024,512]{1,0:T(8,128)(2,1)S(1)} %get-tuple-element.20), channel_id=1, source_target_pairs={{0,1},{1,2},{2,3},{3,0},{4,5},{5,6},{6,7},{7,4},{8,9},{9,10},{10,1... | collective-permute-start | bytes 3145736 | tf_op jit(solution)/shard_map/ppermute | solution.py:17
  140.1 5.1 %collective-permute-start.4 = (f32[512]{0:T(512)S(1)}, f32[512]{0:T(512)S(1)}, u32[]{:S(2)}, u32[]{:S(2)}) collective-permute-start(f32[512]{0:T(512)S(1)} %broadcast_maximum_fusion), channel_id=1, source_target_pairs={{0,4},{4,8},{8,12},{12,16},{16,20},{20,24},{24,28},{28,0},{1,5},{5... | collective-permute-start | bytes 6152 | tf_op jit(solution)/shard_map/ppermute | solution.py:17
  140.4 5.6 %collective-permute-start.32 = (f32[512]{0:T(512)S(1)}, f32[512]{0:T(512)S(1)}, u32[]{:S(2)}, u32[]{:S(2)}) collective-permute-start(f32[512]{0:T(512)S(1)} %get-tuple-element.23), channel_id=1, source_target_pairs={{0,4},{4,8},{8,12},{12,16},{16,20},{20,24},{24,28},{28,0},{1,5},{5... | collective-permute-start | bytes 6152 | tf_op jit(solution)/shard_map/ppermute | solution.py:17
  142.9 27.8 %collective-permute-start.14 = (bf16[1024,512]{1,0:T(8,128)(2,1)S(1)}, bf16[1024,512]{1,0:T(8,128)(2,1)S(1)}, u32[]{:S(2)}, u32[]{:S(2)}) collective-permute-start(bf16[1024,512]{1,0:T(8,128)(2,1)S(1)} %collective-permute-done.8), channel_id=1, source_target_pairs={{0,1},{1,2},{2,3},{3,0},{4,5},{5,6},{6,7},{7,4},{8,9},{9,10},{10,1... | collective-permute-start | bytes 3145736 | tf_op jit(solution)/shard_map/ppermute | solution.py:17
  145.2 6.7 %collective-permute-start.26 = (f32[512,128]{1,0:T(8,128)S(1)}, f32[512,128]{1,0:T(8,128)S(1)}, u32[]{:S(2)}, u32[]{:S(2)}) collective-permute-start(f32[512,128]{1,0:T(8,128)S(1)} %convolution_add_fusion.2), channel_id=1, source_target_pairs={{0,4},{4,8},{8,12},{12,16},{16,20},{20,24},{24,28},{28,0},{1,5},{5... | collective-permute-start | bytes 786440 | tf_op jit(solution)/shard_map/ppermute | solution.py:17
  145.9 25.9 %collective-permute-start.13 = (bf16[512,512]{1,0:T(8,128)(2,1)}, bf16[512,512]{1,0:T(8,128)(2,1)S(1)}, u32[]{:S(2)}, u32[]{:S(2)}) collective-permute-start(bf16[512,512]{1,0:T(8,128)(2,1)} %collective-permute-done.7), channel_id=1, source_target_pairs={{0,4},{4,8},{8,12},{12,16},{16,20},{20,24},{24,28},{28,0},{1,5},{5... | collective-permute-start | bytes 1572872 | tf_op jit(solution)/shard_map/ppermute | solution.py:17
  146.7 24.3 %collective-permute-start.12 = (f32[512]{0:T(512)S(1)}, f32[512]{0:T(512)S(1)}, u32[]{:S(2)}, u32[]{:S(2)}) collective-permute-start(f32[512]{0:T(512)S(1)} %collective-permute-done.6), channel_id=1, source_target_pairs={{0,4},{4,8},{8,12},{12,16},{16,20},{20,24},{24,28},{28,0},{1,5},{5... | collective-permute-start | bytes 6152 | tf_op jit(solution)/shard_map/ppermute | solution.py:17
  146.9 53.1 %collective-permute-start.21 = (f32[512]{0:T(512)S(1)}, f32[512]{0:T(512)S(1)}, u32[]{:S(2)}, u32[]{:S(2)}) collective-permute-start(f32[512]{0:T(512)S(1)} %collective-permute-done.15), channel_id=1, source_target_pairs={{0,4},{4,8},{8,12},{12,16},{16,20},{20,24},{24,28},{28,0},{1,5},{5... | collective-permute-start | bytes 6152 | tf_op jit(solution)/shard_map/ppermute | solution.py:17
  151.9 24.3 %collective-permute-start.29 = (bf16[1024,128]{1,0:T(8,128)(2,1)S(1)}, bf16[1024,128]{1,0:T(8,128)(2,1)S(1)}, u32[]{:S(2)}, u32[]{:S(2)}) collective-permute-start(bf16[1024,128]{1,0:T(8,128)(2,1)S(1)} %collective-permute-done.27), channel_id=1, source_target_pairs={{0,1},{1,2},{2,3},{3,0},{4,5},{5,6},{6,7},{7,4},{8,9},{9,10},{10,1... | collective-permute-start | bytes 786440 | tf_op jit(solution)/shard_map/ppermute | solution.py:17
  170.7 3.9 %collective-permute-start.10 = (f32[512]{0:T(512)S(1)}, f32[512]{0:T(512)S(1)}, u32[]{:S(2)}, u32[]{:S(2)}) collective-permute-start(f32[512]{0:T(512)S(1)} %max.9), channel_id=1, source_target_pairs={{0,4},{4,8},{8,12},{12,16},{16,20},{20,24},{24,28},{28,0},{1,5},{5... | collective-permute-start | bytes 6152 | tf_op jit(solution)/shard_map/ppermute | solution.py:17
  171.0 4.3 %collective-permute-start.33 = (f32[512]{0:T(512)S(1)}, f32[512]{0:T(512)S(1)}, u32[]{:S(2)}, u32[]{:S(2)}) collective-permute-start(f32[512]{0:T(512)S(1)} %get-tuple-element.9), channel_id=1, source_target_pairs={{0,4},{4,8},{8,12},{12,16},{16,20},{20,24},{24,28},{28,0},{1,5},{5... | collective-permute-start | bytes 6152 | tf_op jit(solution)/shard_map/ppermute | solution.py:17
  171.9 27.8 %collective-permute-start.20 = (bf16[1024,512]{1,0:T(8,128)(2,1)S(1)}, bf16[1024,512]{1,0:T(8,128)(2,1)S(1)}, u32[]{:S(2)}, u32[]{:S(2)}) collective-permute-start(bf16[1024,512]{1,0:T(8,128)(2,1)S(1)} %collective-permute-done.14), channel_id=1, source_target_pairs={{0,1},{1,2},{2,3},{3,0},{4,5},{5,6},{6,7},{7,4},{8,9},{9,10},{10,1... | collective-permute-start | bytes 3145736 | tf_op jit(solution)/shard_map/ppermute | solution.py:17
  174.6 6.7 %collective-permute-start.28 = (f32[512,128]{1,0:T(8,128)S(1)}, f32[512,128]{1,0:T(8,128)S(1)}, u32[]{:S(2)}, u32[]{:S(2)}) collective-permute-start(f32[512,128]{1,0:T(8,128)S(1)} %multiply_add_fusion), channel_id=1, source_target_pairs={{0,4},{4,8},{8,12},{12,16},{16,20},{20,24},{24,28},{28,0},{1,5},{5... | collective-permute-start | bytes 786440 | tf_op jit(solution)/shard_map/ppermute | solution.py:17
  175.3 27.1 %collective-permute-start.19 = (bf16[512,512]{1,0:T(8,128)(2,1)S(1)}, bf16[512,512]{1,0:T(8,128)(2,1)S(1)}, u32[]{:S(2)}, u32[]{:S(2)}) collective-permute-start(bf16[512,512]{1,0:T(8,128)(2,1)S(1)} %collective-permute-done.13), channel_id=1, source_target_pairs={{0,4},{4,8},{8,12},{12,16},{16,20},{20,24},{24,28},{28,0},{1,5},{5... | collective-permute-start | bytes 1572872 | tf_op jit(solution)/shard_map/ppermute | solution.py:17
  176.2 26.2 %collective-permute-start.18 = (f32[512]{0:T(512)S(1)}, f32[512]{0:T(512)S(1)}, u32[]{:S(2)}, u32[]{:S(2)}) collective-permute-start(f32[512]{0:T(512)S(1)} %collective-permute-done.12), channel_id=1, source_target_pairs={{0,4},{4,8},{8,12},{12,16},{16,20},{20,24},{24,28},{28,0},{1,5},{5... | collective-permute-start | bytes 6152 | tf_op jit(solution)/shard_map/ppermute | solution.py:17
  181.3 23.1 %collective-permute-start.31 = (bf16[1024,128]{1,0:T(8,128)(2,1)S(1)}, bf16[1024,128]{1,0:T(8,128)(2,1)S(1)}, u32[]{:S(2)}, u32[]{:S(2)}) collective-permute-start(bf16[1024,128]{1,0:T(8,128)(2,1)S(1)} %collective-permute-done.29), channel_id=1, source_target_pairs={{0,1},{1,2},{2,3},{3,0},{4,5},{5,6},{6,7},{7,4},{8,9},{9,10},{10,1... | collective-permute-start | bytes 786440 | tf_op jit(solution)/shard_map/ppermute | solution.py:17
  199.7 3.9 %collective-permute-start.16 = (f32[512]{0:T(512)S(1)}, f32[512]{0:T(512)S(1)}, u32[]{:S(2)}, u32[]{:S(2)}) collective-permute-start(f32[512]{0:T(512)S(1)} %max.10), channel_id=1, source_target_pairs={{0,4},{4,8},{8,12},{12,16},{16,20},{20,24},{24,28},{28,0},{1,5},{5... | collective-permute-start | bytes 6152 | tf_op jit(solution)/shard_map/ppermute | solution.py:17
  200.0 4.3 %collective-permute-start.34 = (f32[512]{0:T(512)S(1)}, f32[512]{0:T(512)S(1)}, u32[]{:S(2)}, u32[]{:S(2)}) collective-permute-start(f32[512]{0:T(512)S(1)} %get-tuple-element.7), channel_id=1, source_target_pairs={{0,4},{4,8},{8,12},{12,16},{16,20},{20,24},{24,28},{28,0},{1,5},{5... | collective-permute-start | bytes 6152 | tf_op jit(solution)/shard_map/ppermute | solution.py:17
  202.3 6.7 %collective-permute-start.30 = (f32[512,128]{1,0:T(8,128)S(1)}, f32[512,128]{1,0:T(8,128)S(1)}, u32[]{:S(2)}, u32[]{:S(2)}) collective-permute-start(f32[512,128]{1,0:T(8,128)S(1)} %convolution_add_fusion.1), channel_id=1, source_target_pairs={{0,4},{4,8},{8,12},{12,16},{16,20},{20,24},{24,28},{28,0},{1,5},{5... | collective-permute-start | bytes 786440 | tf_op jit(solution)/shard_map/ppermute | solution.py:17
  209.7 5.8 %collective-permute-start.35 = (f32[512,128]{1,0:T(8,128)S(1)}, f32[512,128]{1,0:T(8,128)S(1)}, u32[]{:S(2)}, u32[]{:S(2)}) collective-permute-start(f32[512,128]{1,0:T(8,128)S(1)} %fusion.9), channel_id=1, source_target_pairs={{0,20},{4,24},{8,28},{12,0},{16,4},{20,8},{24,12},{28,16},{1,21},{... | collective-permute-start | bytes 786440 | tf_op jit(solution)/shard_map/ppermute | solution.py:17
where the time goes:
time: 216 us
  waiting for transfers between devices  168 us (78%)
  starting transfers between devices  19.2 us (9%)
  matrix products  9.26 us (4%)
  local copies, waits for them, and re-layouts  6.88 us (3%)
  other arithmetic  6.79 us (3%)
  between operations  5.65 us (3%)
    ppermute x36, waiting for transfers between devices, shifted(): return lax.ppermute(value, axis, pairs)  168 us
    ppermute x36, starting transfers between devices, shifted(): return lax.ppermute(value, axis, pairs)  19.2 us
    dot_general x4, matrix products, visit(): lax.dot_general(queries, references, (((1,), (1,)), ((), ())), preferred_...  6.82 us
  transfers between devices with their start and end apart: 36, of which 14 were waited for; matrix products, arithmetic and copies ran while one was open for 9% of the time, Pallas kernels for 0%

commit v1 on v0

v1 whole, which is shorter than its diff:
```python
import functools

import jax
import jax.numpy as jnp
from jax import lax
from jax.experimental import pallas as pl
from jax.experimental.pallas import tpu as pltpu
from jax.sharding import PartitionSpec as P

STEPS = 4
CHUNKS = 4
REF_PIECE = 256
STAT_ROWS = 16
EPSILON = 1e-06
FLOOR = -1e30
LOW = -1e29
MESH = pl.DeviceIdType.MESH
NT = (((1,), (1,)), ((), ()))


def dequantize(values, scales):
    groups = scales.shape[1]
    width = values.shape[1] // groups
    wide = values.astype(jnp.float32)
    parts = [
        (wide[:, g * width : (g + 1) * width] * scales[:, g : g + 1]).astype(jnp.bfloat16)
        for g in range(groups)
    ]
    return jnp.concatenate(parts, axis=1)


def split_squares(matrix):
    square = jnp.square(matrix.astype(jnp.float32))
    high = square.astype(jnp.bfloat16)
    return high, (square - high.astype(jnp.float32)).astype(jnp.bfloat16)


def split_three(value):
    high = value.astype(jnp.bfloat16).astype(jnp.float32)
    rest = value - high
    middle = rest.astype(jnp.bfloat16).astype(jnp.float32)
    return [high, middle, rest - middle]


def kernel(
    n_pb,
    n_row,
    query_emb,
    query_scales,
    sharpness,
    ref_emb,
    ref_scales,
    properties,
    band_mask,
    ref_skew,
    out,
    refs,
    ref_sq,
    props_t,
    scores,
    aux_own,
    aux_in,
    aux_stage,
    aux_z,
    aux_x_send,
    aux_x_recv,
    aux_z_send,
    aux_z_recv,
    x_send,
    x_recv,
    z_send,
    z_recv,
    rz_send,
    rz_recv,
    rx_send,
    rx_recv,
    *buffers,
):
    place = lax.axis_index("pb")
    slot = lax.axis_index("row")
    chunks = CHUNKS
    queries_in = buffers[0:chunks]
    queries_stage = buffers[chunks : 2 * chunks]
    queries_z = buffers[2 * chunks : 3 * chunks]
    made = buffers[3 * chunks : 4 * chunks]
    returned = buffers[4 * chunks : 5 * chunks]
    passed = buffers[5 * chunks : 6 * chunks]
    finished = buffers[6 * chunks : 7 * chunks]

    query_total, width = query_emb.shape
    ref_total = ref_emb.shape[0]
    rows = query_total // chunks
    tile_rows = query_total // band_mask.shape[0]
    query_tiles = query_total // tile_rows
    ref_tiles = ref_total // tile_rows
    prop_width = properties.shape[1]

    def at_pb(steps):
        return (lax.rem(place + n_pb + steps, n_pb), slot)

    def at_row(steps):
        return (place, lax.rem(slot + n_row + steps, n_row))

    partners = [at_pb(t) for t in range(1, STEPS)] + [at_pb(-t) for t in range(1, STEPS)]
    partners += [at_row(d) for d in range(1, n_row)]
    barrier = pltpu.get_barrier_semaphore()
    for partner in partners:
        pl.semaphore_signal(barrier, inc=1, device_id=partner, device_id_type=MESH)

    def remote(source, target, send, recv, device):
        return pltpu.make_async_remote_copy(
            src_ref=source,
            dst_ref=target,
            send_sem=send,
            recv_sem=recv,
            device_id=device,
            device_id_type=MESH,
        )

    def aux_x(t):
        return remote(
            aux_own.at[t], aux_in.at[t], aux_x_send.at[t], aux_x_recv.at[t], at_pb(t)
        )

    def aux_to_z(d):
        return remote(
            aux_stage.at[d], aux_z.at[d], aux_z_send.at[d], aux_z_recv.at[d], at_row(d)
        )

    def go_x(c, t):
        k = c * STEPS + t
        return remote(
            queries_in[c].at[0], queries_in[c].at[t], x_send.at[k], x_recv.at[k], at_pb(t)
        )

    def go_z(c, d):
        k = c * n_row + d
        return remote(
            queries_stage[c].at[d], queries_z[c].at[d], z_send.at[k], z_recv.at[k], at_row(d)
        )

    def back_z(c, d):
        k = c * n_row + d
        return remote(
            made[c].at[d], returned[c].at[d], rz_send.at[k], rz_recv.at[k], at_row(-d)
        )

    def back_x(c, t):
        k = c * STEPS + t
        return remote(
            passed[c].at[t], finished[c].at[t], rx_send.at[k], rx_recv.at[k], at_pb(-t)
        )

    own_skew = ref_skew[place]

    def turned(steps):
        return lax.rem(2 * n_row - steps - own_skew, n_row)

    def visit_of(d):
        return jnp.minimum(turned(d), STEPS - 1)

    ones = jnp.ones((8, width), jnp.bfloat16)
    for c in range(chunks):
        part = pl.ds(c * rows, rows)
        queries_in[c][0] = dequantize(query_emb[part, :], query_scales[part, :])
        if c == 0:
            pl.semaphore_wait(barrier, len(partners))
        for t in range(STEPS - 1, 0, -1):
            go_x(c, t).start()
    lanes = lax.broadcasted_iota(jnp.int32, (1, query_total), 1) // tile_rows
    squares = []
    for c in range(chunks):
        high, low = split_squares(queries_in[c][0])
        squares.append(
            (
                lax.dot_general(ones, high, NT, preferred_element_type=jnp.float32)
                + lax.dot_general(ones, low, NT, preferred_element_type=jnp.float32)
            )[0:1]
        )
    query_sq = jnp.concatenate(squares, axis=1)
    for t in range(STEPS):
        group = lax.rem(place + t, n_pb)
        row_slot = lax.rem(slot - ref_skew[group] - t + 8 * n_row, n_row)
        first = (group * n_row + row_slot) * ref_tiles
        lines = [sharpness[...], query_sq]
        for j in range(ref_tiles):
            line = jnp.zeros((1, query_total), jnp.float32)
            for i in range(query_tiles):
                bias = jnp.where(band_mask[i, first + j] == 1, 0.0, FLOOR)
                line = jnp.where(lanes == i, bias, line)
            lines.append(line)
        lines.append(jnp.zeros((8 - len(lines), query_total), jnp.float32))
        (aux_in.at[0] if t == 0 else aux_own.at[t])[...] = jnp.concatenate(lines, axis=0)
        if t > 0:
            aux_x(t).start()

    ones_ref = jnp.ones((rows, width), jnp.bfloat16)

    def prepare(i, _):
        part = pl.ds(pl.multiple_of(i * REF_PIECE, REF_PIECE), REF_PIECE)
        block = dequantize(ref_emb[part, :], ref_scales[part, :])
        refs[part, :] = block
        high, low = split_squares(block)
        ref_sq[part, :] = (
            lax.dot_general(high, ones_ref, NT, preferred_element_type=jnp.float32)
            + lax.dot_general(low, ones_ref, NT, preferred_element_type=jnp.float32)
            + EPSILON
        )
        return 0

    lax.fori_loop(0, ref_total // REF_PIECE, prepare, 0)
    for j in range(ref_total // REF_PIECE):
        part = pl.ds(j * REF_PIECE, REF_PIECE)
        props_t[:, part] = properties[part, :].astype(jnp.float32).T.astype(jnp.bfloat16)

    def distribute(c):
        if c == 0:
            for t in range(1, STEPS):
                aux_x(t).wait_recv()
            for d in range(1, n_row):
                aux_stage[d] = aux_in[visit_of(d)]
                aux_to_z(d).start()
            aux_z[0] = aux_in[visit_of(0)]
        for t in range(1, STEPS):
            go_x(c, t).wait_recv()
        for d in range(1, n_row):
            queries_stage[c][d] = queries_in[c][visit_of(d)]
            go_z(c, d).start()
        queries_z[c][0] = queries_in[c][visit_of(0)]

    def attend(c, d):
        queries = queries_z[c][d]
        columns = slice(c * rows, (c + 1) * rows)
        sharpen = aux_z[d, 0:1, columns]
        own_sq = aux_z[d, 1:2, columns]
        top = jnp.full((1, rows), LOW, jnp.float32)
        for j in range(ref_tiles):
            part = slice(j * tile_rows, (j + 1) * tile_rows)
            inner = lax.dot_general(
                refs[part, :], queries, NT, preferred_element_type=jnp.float32
            )
            score = sharpen * inner / (ref_sq[part, :] + own_sq - inner)
            score = score + aux_z[d, 2 + j : 3 + j, columns]
            scores[part, :] = score
            top = jnp.maximum(top, jnp.max(score, axis=0, keepdims=True))
        total = jnp.zeros((1, rows), jnp.float32)
        weighted = jnp.zeros((prop_width, rows), jnp.float32)
        for j in range(ref_tiles):
            part = slice(j * tile_rows, (j + 1) * tile_rows)
            weights = jnp.exp(scores[part, :] - top)
            total = total + jnp.sum(weights, axis=0, keepdims=True)
            weighted = weighted + jnp.dot(
                props_t[:, part], weights.astype(jnp.bfloat16), preferred_element_type=jnp.float32
            )
        stats = split_three(top) + split_three(total)
        stats.append(jnp.zeros((STAT_ROWS - len(stats), rows), jnp.float32))
        return weighted.astype(jnp.bfloat16), jnp.concatenate(stats, axis=0).astype(jnp.bfloat16)

    def work(c):
        if c == 0:
            for d in range(1, n_row):
                aux_to_z(d).wait_recv()

        def one(d, _):
            @pl.when(d > 0)
            def _():
                go_z(c, d).wait_recv()

            weighted, stats = attend(c, d)
            made[c][d, 0:prop_width, :] = weighted
            made[c][d, prop_width:, :] = stats

            @pl.when(d > 0)
            def _():
                back_z(c, d).start()

            return 0

        lax.fori_loop(0, n_row, one, 0)
        returned[c][0] = made[c][0]

    def collect(c):
        for d in range(1, n_row):
            back_z(c, d).wait_recv()
        for t in range(STEPS - 1, 0, -1):
            passed[c][t] = returned[c][turned(t)]
            back_x(c, t).start()
        finished[c][0] = returned[c][turned(0)]

    def finish(c):
        for t in range(1, STEPS):
            back_x(c, t).wait_recv()
        tops, totals = [], []
        for t in range(STEPS):
            stats = finished[c][t, prop_width:, :].astype(jnp.float32)
            tops.append(stats[0:1] + stats[1:2] + stats[2:3])
            totals.append(stats[3:4] + stats[4:5] + stats[5:6])
        top = functools.reduce(jnp.maximum, tops)
        total = jnp.zeros((1, rows), jnp.float32)
        weighted = jnp.zeros((prop_width, rows), jnp.float32)
        for t in range(STEPS):
            rescale = jnp.exp(tops[t] - top)
            total = total + rescale * totals[t]
            weighted = weighted + rescale * finished[c][t, 0:prop_width, :].astype(jnp.float32)
        out[c * rows : (c + 1) * rows, :] = (weighted / total).T

    for step in range(chunks + 3):
        if step < chunks:
            distribute(step)
        if 0 <= step - 1 < chunks:
            work(step - 1)
        if 0 <= step - 2 < chunks:
            collect(step - 2)
        if 0 <= step - 3 < chunks:
            finish(step - 3)

    for t in range(1, STEPS):
        aux_x(t).wait_send()
    for d in range(1, n_row):
        aux_to_z(d).wait_send()
    for c in range(chunks):
        for t in range(1, STEPS):
            go_x(c, t).wait_send()
            back_x(c, t).wait_send()
        for d in range(1, n_row):
            go_z(c, d).wait_send()
            back_z(c, d).wait_send()


def local(query_emb, query_scales, sharpness, ref_emb, ref_scales, properties, band_mask, ref_skew):
    n_pb = lax.axis_size("pb")
    n_row = lax.axis_size("row")
    query_total, width = query_emb.shape
    ref_total = ref_emb.shape[0]
    prop_width = properties.shape[1]
    rows = query_total // CHUNKS
    low = jnp.bfloat16
    packed = (prop_width + STAT_ROWS, rows)
    kinds = [
        (STEPS, rows, width),
        (n_row, rows, width),
        (n_row, rows, width),
        (n_row,) + packed,
        (n_row,) + packed,
        (STEPS,) + packed,
        (STEPS,) + packed,
    ]
    vmem = pl.BlockSpec(memory_space=pltpu.VMEM)
    smem = pl.BlockSpec(memory_space=pltpu.SMEM)
    dma = pltpu.SemaphoreType.DMA
    sems = [STEPS, STEPS, n_row, n_row]
    sems += [CHUNKS * STEPS] * 2 + [CHUNKS * n_row] * 4 + [CHUNKS * STEPS] * 2
    pairs = STEPS * query_total * ref_total
    return pl.pallas_call(
        functools.partial(kernel, n_pb, n_row),
        out_shape=jax.ShapeDtypeStruct((query_total, prop_width), jnp.float32),
        in_specs=[vmem] * 6 + [smem] * 2,
        out_specs=vmem,
        scratch_shapes=[
            pltpu.VMEM((ref_total, width), low),
            pltpu.VMEM((ref_total, rows), jnp.float32),
            pltpu.VMEM((prop_width, ref_total), low),
            pltpu.VMEM((ref_total, rows), jnp.float32),
            pltpu.VMEM((STEPS, 8, query_total), jnp.float32),
            pltpu.VMEM((STEPS, 8, query_total), jnp.float32),
            pltpu.VMEM((n_row, 8, query_total), jnp.float32),
            pltpu.VMEM((n_row, 8, query_total), jnp.float32),
        ]
        + [dma((count,)) for count in sems]
        + [pltpu.VMEM(kind, low) for kind in kinds for _ in range(CHUNKS)],
        compiler_params=pltpu.CompilerParams(
            collective_id=0, has_side_effects=True, vmem_limit_bytes=56 * 1024 * 1024
        ),
        cost_estimate=pl.CostEstimate(
            flops=2 * pairs * (width + prop_width),
            bytes_accessed=4 * 1024 * 1024,
            transcendentals=2 * pairs,
        ),
    )(
        query_emb,
        query_scales,
        sharpness.reshape(1, query_total),
        ref_emb,
        ref_scales,
        properties,
        band_mask,
        ref_skew,
    )


def solution(mesh):
    placed = (
        P(("pb", "row"), None),
        P(("pb", "row"), None),
        P(("pb", "row")),
        P(("pb", "row"), None),
        P(("pb", "row"), None),
        P(("pb", "row"), None),
        P(("pb", "row"), None),
        P(),
    )
    return jax.shard_map(
        local, mesh=mesh, in_specs=placed, out_specs=P(("pb", "row"), None), check_vma=False
    )
```

time: 216 us -> 106 us (0.49)
  waiting for transfers between devices: 168 us -> 0 us
  Pallas kernels: 0 us -> 101 us
  starting transfers between devices: 19.2 us -> 0 us
  matrix products: 9.26 us -> 0 us
  other arithmetic: 6.79 us -> 0 us
  between operations: 5.65 us -> 0.01 us
  local copies, waits for them, and re-layouts: 6.88 us -> 4.25 us
    ppermute x36 -> x0, waiting for transfers between devices: 168 us -> none  [shifted(): return lax.ppermute(value, axis, pairs)]
    pallas_call x0 -> x1, Pallas kernels: none -> 101 us  [local(): pl.pallas_call(functools.partial(kernel, n_pb, n_row), out_shape=jax.Shap...]
    ppermute x36 -> x0, starting transfers between devices: 19.2 us -> none  [shifted(): return lax.ppermute(value, axis, pairs)]
    dot_general x8 -> x0, matrix products: 9.26 us -> none  [the longest x4 6.82 us: visit(): lax.dot_general(queries, references, (((1,), (1,)), ((), ())), preferred_...]
    reduce_sum x9 -> x0, other arithmetic: 5.83 us -> none  [the longest x5 3.24 us: squares(): return jnp.sum(jnp.square(matrix.astype(jnp.float32)), axis=1)]
  transfers between devices with their start and end apart: 36 -> 0, of which waited for: 14 -> 0; matrix products, arithmetic and copies ran while one was open for 9% -> 0% of each run, Pallas kernels for 0% -> 0%
where the time goes in v1:
time: 106 us
  Pallas kernels  101 us (95%)
  local copies, waits for them, and re-layouts  4.25 us (4%)
    pallas_call x1, Pallas kernels, local(): pl.pallas_call(functools.partial(kernel, n_pb, n_row), out_shape=jax.Shap...  101 us
    unnamed x5, local copies, waits for them, and re-layouts  4.25 us

profile of v1, /device:TPU:0, one launch (start us, length us, event | category | flops | bytes accessed | tf_op | source)
XLA Modules:
  0.0 105.7 jit_solution(5544217742319405681)
XLA Ops:
  0.0 0.0 copy-start
  0.0 1.6 %copy.9.query_scales = f32[512,4]{1,0:T(8,128)} copy(f32[512,4]{0,1:T(4,128)} %param.9) | data formatting | bytes 16384 | tf_op args[1]
  1.6 0.0 copy-done
  1.6 1.0 copy.10.ref_scales
  2.6 101.4 %shard_map.82 = f32[512,128]{1,0:T(8,128)} custom-call(bf16[512,512]{1,0:T(8,128)(2,1)} %query_emb.1, f32[512,4]{1,0:T(8,128)} %copy.9.query_scales, f32[1,512]{1,0:T(1,128)} %bitcast.1, bf16[1024,512]{1,0:T(8,128)(2,1)} %ref_emb.1, f32[1024,4]{1,0:T(8,128)} %copy.10.ref_scales, bf16[1024,128]{1,0:T(8,128)(2,1)} %properties.1, s32[2,128]{1,0:T(2,128)} %band_mask.1, ...), custom_call_target="tpu_custom_call" | custom-call | flops 2684354560 | bytes 4194304 | tf_op jit(solution)/shard_map/pallas_call | solution.py:354
  104.0 1.7 %copy.12 = f32[512,128]{1,0:T(8,128)} copy(f32[512,128]{1,0:T(8,128)} %shard_map.82) | data formatting | bytes 524288
Async XLA Ops:
  0.0 1.6 %copy-start = (f32[1024,4]{0,1:T(4,128)S(1)}, f32[1024,4]{0,1:T(4,128)}, u32[]{:S(2)}) copy-start(f32[1024,4]{0,1:T(4,128)} %param.12) | copy-start | bytes 49156

commit v2 on v1

--- a/solution.py
+++ b/solution.py
@@ -19,7 +19,8 @@
 
 
 def dequantize(values, scales):
-    groups = scales.shape[1]
+    groups = scales.shape[0]
+    scales = jnp.concatenate([scales, jnp.zeros((8 - groups, scales.shape[1]), jnp.float32)], axis=0).T
     width = values.shape[1] // groups
     wide = values.astype(jnp.float32)
     parts = [
@@ -68,8 +69,10 @@
     aux_z_recv,
     x_send,
     x_recv,
-    z_send,
-    z_recv,
+    up_send,
+    up_recv,
+    down_send,
+    down_recv,
     rz_send,
     rz_recv,
     rx_send,
@@ -79,9 +82,9 @@
     place = lax.axis_index("pb")
     slot = lax.axis_index("row")
     chunks = CHUNKS
-    queries_in = buffers[0:chunks]
+    gathered = buffers[0:chunks]
     queries_stage = buffers[chunks : 2 * chunks]
-    queries_z = buffers[2 * chunks : 3 * chunks]
+    queries_in = buffers[2 * chunks : 3 * chunks]
     made = buffers[3 * chunks : 4 * chunks]
     returned = buffers[4 * chunks : 5 * chunks]
     passed = buffers[5 * chunks : 6 * chunks]
@@ -130,14 +133,56 @@
     def go_x(c, t):
         k = c * STEPS + t
         return remote(
-            queries_in[c].at[0], queries_in[c].at[t], x_send.at[k], x_recv.at[k], at_pb(t)
-        )
-
-    def go_z(c, d):
-        k = c * n_row + d
-        return remote(
-            queries_stage[c].at[d], queries_z[c].at[d], z_send.at[k], z_recv.at[k], at_row(d)
-        )
+            queries_stage[c].at[t], queries_in[c].at[t], x_send.at[k], x_recv.at[k], at_pb(t)
+        )
+
+    def go_up(c, h):
+        block = gathered[c].at[lax.rem(slot + n_row - h, n_row)]
+        k = c * n_row + h
+        return remote(block, block, up_send.at[k], up_recv.at[k], at_row(1))
+
+    def go_down(c, h):
+        block = gathered[c].at[lax.rem(slot + h, n_row)]
+        k = c * n_row + h
+        return remote(block, block, down_send.at[k], down_recv.at[k], at_row(-1))
+
+    def from_below(c, h):
+        block = gathered[c].at[lax.rem(slot + n_row - h, n_row)]
+        k = c * n_row + h - 1
+        return remote(block, block, up_send.at[k], up_recv.at[k], at_row(1))
+
+    def from_above(c, h):
+        block = gathered[c].at[lax.rem(slot + h, n_row)]
+        k = c * n_row + h - 1
+        return remote(block, block, down_send.at[k], down_recv.at[k], at_row(-1))
+
+    def hop(c, h):
+        @pl.when(slot >= h)
+        def _():
+            if h > 0:
+                from_below(c, h).wait_recv()
+
+            @pl.when(slot < n_row - 1)
+            def _():
+                go_up(c, h).start()
+
+        @pl.when(slot + h < n_row)
+        def _():
+            if h > 0:
+                from_above(c, h).wait_recv()
+
+            @pl.when(slot > 0)
+            def _():
+                go_down(c, h).start()
+
+    def sent(c, h):
+        @pl.when((slot >= h) & (slot < n_row - 1))
+        def _():
+            go_up(c, h).wait_send()
+
+        @pl.when((slot + h < n_row) & (slot > 0))
+        def _():
+            go_down(c, h).wait_send()
 
     def back_z(c, d):
         k = c * n_row + d
@@ -162,15 +207,14 @@
     ones = jnp.ones((8, width), jnp.bfloat16)
     for c in range(chunks):
         part = pl.ds(c * rows, rows)
-        queries_in[c][0] = dequantize(query_emb[part, :], query_scales[part, :])
+        gathered[c][slot] = dequantize(query_emb[part, :], query_scales[:, part])
         if c == 0:
             pl.semaphore_wait(barrier, len(partners))
-        for t in range(STEPS - 1, 0, -1):
-            go_x(c, t).start()
+            hop(0, 0)
     lanes = lax.broadcasted_iota(jnp.int32, (1, query_total), 1) // tile_rows
     squares = []
     for c in range(chunks):
-        high, low = split_squares(queries_in[c][0])
+        high, low = split_squares(gathered[c][slot])
         squares.append(
             (
                 lax.dot_general(ones, high, NT, preferred_element_type=jnp.float32)
@@ -198,7 +242,7 @@
 
     def prepare(i, _):
         part = pl.ds(pl.multiple_of(i * REF_PIECE, REF_PIECE), REF_PIECE)
-        block = dequantize(ref_emb[part, :], ref_scales[part, :])
+        block = dequantize(ref_emb[part, :], ref_scales[:, part])
         refs[part, :] = block
         high, low = split_squares(block)
         ref_sq[part, :] = (
@@ -213,23 +257,26 @@
         part = pl.ds(j * REF_PIECE, REF_PIECE)
         props_t[:, part] = properties[part, :].astype(jnp.float32).T.astype(jnp.bfloat16)
 
+    def distribute_aux():
+        for t in range(1, STEPS):
+            aux_x(t).wait_recv()
+        for d in range(1, n_row):
+            aux_stage[d] = aux_in[visit_of(d)]
+            aux_to_z(d).start()
+        aux_z[0] = aux_in[visit_of(0)]
+
     def distribute(c):
-        if c == 0:
-            for t in range(1, STEPS):
-                aux_x(t).wait_recv()
-            for d in range(1, n_row):
-                aux_stage[d] = aux_in[visit_of(d)]
-                aux_to_z(d).start()
-            aux_z[0] = aux_in[visit_of(0)]
-        for t in range(1, STEPS):
-            go_x(c, t).wait_recv()
-        for d in range(1, n_row):
-            queries_stage[c][d] = queries_in[c][visit_of(d)]
-            go_z(c, d).start()
-        queries_z[c][0] = queries_in[c][visit_of(0)]
+        for t in range(STEPS):
+            skew = ref_skew[lax.rem(place + t, n_pb)]
+            block = gathered[c][lax.rem(slot + skew + t, n_row)]
+            if t == 0:
+                queries_in[c][0] = block
+            else:
+                queries_stage[c][t] = block
+                go_x(c, t).start()
 
     def attend(c, d):
-        queries = queries_z[c][d]
+        queries = queries_in[c][visit_of(d)]
         columns = slice(c * rows, (c + 1) * rows)
         sharpen = aux_z[d, 0:1, columns]
         own_sq = aux_z[d, 1:2, columns]
@@ -260,12 +307,10 @@
         if c == 0:
             for d in range(1, n_row):
                 aux_to_z(d).wait_recv()
+        for t in range(1, STEPS):
+            go_x(c, t).wait_recv()
 
         def one(d, _):
-            @pl.when(d > 0)
-            def _():
-                go_z(c, d).wait_recv()
-
             weighted, stats = attend(c, d)
             made[c][d, 0:prop_width, :] = weighted
             made[c][d, prop_width:, :] = stats
@@ -304,15 +349,16 @@
             weighted = weighted + rescale * finished[c][t, 0:prop_width, :].astype(jnp.float32)
         out[c * rows : (c + 1) * rows, :] = (weighted / total).T
 
-    for step in range(chunks + 3):
-        if step < chunks:
-            distribute(step)
-        if 0 <= step - 1 < chunks:
-            work(step - 1)
-        if 0 <= step - 2 < chunks:
-            collect(step - 2)
-        if 0 <= step - 3 < chunks:
-            finish(step - 3)
+    for step in range(chunks + n_row + 2):
+        for h in range(n_row):
+            if 0 <= step - h < chunks and step > 0:
+                hop(step - h, h)
+        if step == 1:
+            distribute_aux()
+        for lag, stage in ((0, distribute), (1, work), (2, collect), (3, finish)):
+            c = step - (n_row - 1) - lag
+            if 0 <= c < chunks:
+                stage(c)
 
     for t in range(1, STEPS):
         aux_x(t).wait_send()
@@ -323,8 +369,9 @@
             go_x(c, t).wait_send()
             back_x(c, t).wait_send()
         for d in range(1, n_row):
-            go_z(c, d).wait_send()
             back_z(c, d).wait_send()
+        for h in range(n_row - 1):
+            sent(c, h)
 
 
 def local(query_emb, query_scales, sharpness, ref_emb, ref_scales, properties, band_mask, ref_skew):
@@ -337,9 +384,9 @@
     low = jnp.bfloat16
     packed = (prop_width + STAT_ROWS, rows)
     kinds = [
+        (n_row, rows, width),
         (STEPS, rows, width),
-        (n_row, rows, width),
-        (n_row, rows, width),
+        (STEPS, rows, width),
         (n_row,) + packed,
         (n_row,) + packed,
         (STEPS,) + packed,
@@ -349,7 +396,7 @@
     smem = pl.BlockSpec(memory_space=pltpu.SMEM)
     dma = pltpu.SemaphoreType.DMA
     sems = [STEPS, STEPS, n_row, n_row]
-    sems += [CHUNKS * STEPS] * 2 + [CHUNKS * n_row] * 4 + [CHUNKS * STEPS] * 2
+    sems += [CHUNKS * STEPS] * 2 + [CHUNKS * n_row] * 6 + [CHUNKS * STEPS] * 2
     pairs = STEPS * query_total * ref_total
     return pl.pallas_call(
         functools.partial(kernel, n_pb, n_row),
@@ -378,10 +425,10 @@
         ),
     )(
         query_emb,
-        query_scales,
+        query_scales.T,
         sharpness.reshape(1, query_total),
         ref_emb,
-        ref_scales,
+        ref_scales.T,
         properties,
         band_mask,
         ref_skew,

time: 106 us -> 72.4 us (0.68)
  Pallas kernels: 101 us -> 70.5 us
  local copies, waits for them, and re-layouts: 4.25 us -> 1.67 us
    pallas_call x1, Pallas kernels: 101 us -> 70.5 us  [local(): pl.pallas_call(functools.partial(kernel, n_pb, n_row), out_shape=jax.Shap...]
    unnamed x5 -> x1, local copies, waits for them, and re-layouts: 4.25 us -> 1.67 us
where the time goes in v2:
time: 72.4 us; the launch traced here: 72.2 us
  Pallas kernels  70.5 us (97%)
  local copies, waits for them, and re-layouts  1.67 us (2%)
    pallas_call x1, Pallas kernels, local(): pl.pallas_call(functools.partial(kernel, n_pb, n_row), out_shape=jax.Shap...  70.5 us
    unnamed x1, local copies, waits for them, and re-layouts  1.67 us

profile of v2, /device:TPU:0, one launch (start us, length us, event | category | flops | bytes accessed | tf_op | source)
XLA Modules:
  0.0 72.2 jit_solution(7388914218726750047)
XLA Ops:
  0.0 70.5 %shard_map.82 = f32[512,128]{1,0:T(8,128)} custom-call(bf16[512,512]{1,0:T(8,128)(2,1)} %query_emb.1, f32[4,512]{1,0:T(4,128)} %bitcast.4, f32[1,512]{1,0:T(1,128)} %bitcast.5, bf16[1024,512]{1,0:T(8,128)(2,1)} %ref_emb.1, f32[4,1024]{1,0:T(4,128)} %bitcast.3, bf16[1024,128]{1,0:T(8,128)(2,1)} %properties.1, s32[2,128]{1,0:T(2,128)} %band_mask.1, s32[8]{0:T(128)} %ref_skew.1), custom_call_target="tpu_custom_call" | custom-call | flops 2684354560 | bytes 4194304 | tf_op jit(solution)/shard_map/pallas_call | solution.py:401
  70.5 1.7 %copy.10 = f32[512,128]{1,0:T(8,128)} copy(f32[512,128]{1,0:T(8,128)} %shard_map.82) | data formatting | bytes 524288

commit v3 on v2

--- a/solution.py
+++ b/solution.py
@@ -204,6 +204,25 @@
     def visit_of(d):
         return jnp.minimum(turned(d), STEPS - 1)
 
+    ones_ref = jnp.ones((rows, width), jnp.bfloat16)
+
+    def prepare(i, _):
+        part = pl.ds(pl.multiple_of(i * REF_PIECE, REF_PIECE), REF_PIECE)
+        block = dequantize(ref_emb[part, :], ref_scales[:, part])
+        refs[part, :] = block
+        high, low = split_squares(block)
+        ref_sq[part, :] = (
+            lax.dot_general(high, ones_ref, NT, preferred_element_type=jnp.float32)
+            + lax.dot_general(low, ones_ref, NT, preferred_element_type=jnp.float32)
+            + EPSILON
+        )
+        return 0
+
+    lax.fori_loop(0, ref_total // REF_PIECE, prepare, 0)
+    for j in range(ref_total // REF_PIECE):
+        part = pl.ds(j * REF_PIECE, REF_PIECE)
+        props_t[:, part] = properties[part, :].astype(jnp.float32).T.astype(jnp.bfloat16)
+
     ones = jnp.ones((8, width), jnp.bfloat16)
     for c in range(chunks):
         part = pl.ds(c * rows, rows)
@@ -237,25 +256,6 @@
         (aux_in.at[0] if t == 0 else aux_own.at[t])[...] = jnp.concatenate(lines, axis=0)
         if t > 0:
             aux_x(t).start()
-
-    ones_ref = jnp.ones((rows, width), jnp.bfloat16)
-
-    def prepare(i, _):
-        part = pl.ds(pl.multiple_of(i * REF_PIECE, REF_PIECE), REF_PIECE)
-        block = dequantize(ref_emb[part, :], ref_scales[:, part])
-        refs[part, :] = block
-        high, low = split_squares(block)
-        ref_sq[part, :] = (
-            lax.dot_general(high, ones_ref, NT, preferred_element_type=jnp.float32)
-            + lax.dot_general(low, ones_ref, NT, preferred_element_type=jnp.float32)
-            + EPSILON
-        )
-        return 0
-
-    lax.fori_loop(0, ref_total // REF_PIECE, prepare, 0)
-    for j in range(ref_total // REF_PIECE):
-        part = pl.ds(j * REF_PIECE, REF_PIECE)
-        props_t[:, part] = properties[part, :].astype(jnp.float32).T.astype(jnp.bfloat16)
 
     def distribute_aux():
         for t in range(1, STEPS):

time: 72.4 us -> 71.8 us (level)
  no operation moved by 1% of the time
where the time goes in v3:
time: 71.8 us; the launch traced here: 71.6 us
  Pallas kernels  69.9 us (97%)
  local copies, waits for them, and re-layouts  1.67 us (2%)
    pallas_call x1, Pallas kernels, local(): pl.pallas_call(functools.partial(kernel, n_pb, n_row), out_shape=jax.Shap...  69.9 us
    unnamed x1, local copies, waits for them, and re-layouts  1.67 us

profile of v3, /device:TPU:0, one launch (start us, length us, event | category | flops | bytes accessed | tf_op | source)
XLA Modules:
  0.0 71.6 jit_solution(15451427508748970741)
XLA Ops:
  0.0 69.9 %shard_map.82 = f32[512,128]{1,0:T(8,128)} custom-call(bf16[512,512]{1,0:T(8,128)(2,1)} %query_emb.1, f32[4,512]{1,0:T(4,128)} %bitcast.4, f32[1,512]{1,0:T(1,128)} %bitcast.5, bf16[1024,512]{1,0:T(8,128)(2,1)} %ref_emb.1, f32[4,1024]{1,0:T(4,128)} %bitcast.3, bf16[1024,128]{1,0:T(8,128)(2,1)} %properties.1, s32[2,128]{1,0:T(2,128)} %band_mask.1, s32[8]{0:T(128)} %ref_skew.1), custom_call_target="tpu_custom_call" | custom-call | flops 2684354560 | bytes 4194304 | tf_op jit(solution)/shard_map/pallas_call | solution.py:401
  69.9 1.7 %copy.10 = f32[512,128]{1,0:T(8,128)} copy(f32[512,128]{1,0:T(8,128)} %shard_map.82) | data formatting | bytes 524288
